TPU v7x, 32 devices: a whole 2x2x4 slice. The times are simulated.
32 devices in a mesh: sx: 2 (over x), sy: 4 (over y, core), ta: 4 (over z).
Axes of the slice: x: 2, y: 2, z: 4, core: 2. Of those that a mesh axis runs over, the one named last changes fastest.
Arguments:
- velocity: bfloat16 [3, 256, 8, 1024], P(None, 'ta', 'sx', 'sy'), may hold values from -6 to 6
- seeds_first: int32 [64, 64], replicated, may hold values from -64 to 64
- seeds_merge: int32 [2, 128, 64], replicated, may hold values from -64 to 64
Outputs:
- basis: float32 [64, 5, 8, 1024], P(None, None, 'sx', ('sy', 'ta'))
All inputs are finite; a program needn't handle non-finite values.
Results may differ from a plain program's by a relative error of at most 0.0008.
Values may be sent and summed in bfloat16 or wider, within the bound.
A program may use at most 64 MiB of HBM per device.

v0:
```python
import jax
import jax.numpy as jnp
from jax import lax
from jax.sharding import PartitionSpec as P


def padded_2(x, sides, width):
    for axis, dim in sides:
        size, length = (lax.axis_size(axis), x.shape[dim])
        up = [(i, (i + 1) % size) for i in range(size - 1)]
        down = [(j, i) for i, j in up]
        last = lax.slice_in_dim(x, length - width, length, axis=dim)
        leading = lax.slice_in_dim(x, 0, width, axis=dim)
        before = lax.ppermute(last, axis, up)
        after = lax.ppermute(leading, axis, down)
        x = jnp.concatenate([before, x, after], axis=dim)
    return x


def from_partner(x, axis, apart):
    return lax.ppermute(x, axis, [(i, i ^ 1 << apart) for i in range(lax.axis_size(axis))])


def matmul_hi(left, right):
    return jnp.dot(left, right, precision=lax.Precision.HIGHEST)


def coefficients(gram_mat, rotation):
    order_n = gram_mat.shape[0]
    scaling = jnp.sqrt(jnp.trace(gram_mat) / order_n)
    imaged = matmul_hi(gram_mat, rotation)
    reduced = matmul_hi(rotation.T, imaged)
    factor = jnp.linalg.cholesky(reduced)
    solved = jax.scipy.linalg.solve_triangular(factor, imaged.T, lower=True)
    return solved.T / scaling


def diff_x(field):
    return 0.5 * (field[:, 2:, 1:-1] - field[:, :-2, 1:-1])


def diff_y(field):
    return 0.5 * (field[:, 1:-1, 2:] - field[:, 1:-1, :-2])


def strain_rows(padded):
    comp_u = padded[0]
    comp_v = padded[1]
    comp_w = padded[2]
    fields = jnp.stack(
        [
            diff_x(comp_u),
            diff_y(comp_v),
            0.5 * (diff_y(comp_u) + diff_x(comp_v)),
            0.5 * diff_x(comp_w),
            0.5 * diff_y(comp_w),
        ],
        axis=1,
    )
    return fields.reshape(fields.shape[0], -1)


def rotations(seeds_first, seeds_merge):
    width = seeds_first.shape[0]
    first = jnp.eye(width, dtype=jnp.float32) + seeds_first.astype(jnp.float32) * (
        0.5 / (64.0 * 8.0)
    )
    stacked = jnp.concatenate(
        [jnp.eye(width, dtype=jnp.float32), jnp.eye(width, dtype=jnp.float32)], axis=0
    ) / jnp.sqrt(jnp.float32(2.0))
    merges = stacked[None] + seeds_merge.astype(jnp.float32) * (
        0.5 / (64.0 * jnp.sqrt(jnp.float32(128.0)))
    )
    return (first, merges)


def own_quarter(full_rows, width, cells_x, cells_y, quarter):
    shaped = full_rows.reshape(width, 5, cells_x, cells_y)
    return lax.dynamic_slice_in_dim(shaped, lax.axis_index("ta") * quarter, quarter, 3)


def local(velocity, seeds_first, seeds_merge):
    width = seeds_first.shape[0]
    num_levels = seeds_merge.shape[0]
    cells_x = velocity.shape[2]
    cells_y = velocity.shape[3]
    blocks = lax.axis_size("ta")
    quarter = cells_y // blocks
    rotation_first, rotation_merge = rotations(seeds_first, seeds_merge)
    rimmed = padded_2(velocity, (("sx", 2), ("sy", 3)), 1)
    strain = strain_rows(rimmed.astype(jnp.float32))
    gram_mat = lax.psum(matmul_hi(strain, strain.T), ("sx", "sy"))
    kmat = coefficients(gram_mat, rotation_first)
    basis_now = matmul_hi(kmat.T, strain)
    my_index = lax.axis_index("ta")
    for depth_at in range(num_levels):
        partner = from_partner(basis_now, "ta", depth_at)
        is_upper = my_index // 2**depth_at % 2 == 1
        low_rows = jnp.where(is_upper, partner, basis_now)
        high_rows = jnp.where(is_upper, basis_now, partner)
        gram_low = matmul_hi(low_rows, low_rows.T)
        gram_cross = matmul_hi(low_rows, high_rows.T)
        gram_high = matmul_hi(high_rows, high_rows.T)
        local_pair = jnp.concatenate(
            [
                jnp.concatenate([gram_low, gram_cross], axis=1),
                jnp.concatenate([gram_cross.T, gram_high], axis=1),
            ],
            axis=0,
        )
        pair_total = lax.psum(local_pair, ("sx", "sy"))
        kmat = coefficients(pair_total, rotation_merge[depth_at])
        basis_now = matmul_hi(kmat[:width].T, low_rows) + matmul_hi(kmat[width:].T, high_rows)
    return own_quarter(basis_now, width, cells_x, cells_y, quarter)


def solution(mesh):
    in_specs = (P(None, "ta", "sx", "sy"), P(), P())
    out_specs = P(None, None, "sx", ("sy", "ta"))
    return jax.shard_map(local, mesh=mesh, in_specs=in_specs, out_specs=out_specs, check_vma=False)
```

profile of v0, /device:TPU:0, one launch (start us, length us, event | category | flops | bytes accessed | tf_op | source)
XLA Modules:
  0.0 324.5 jit_solution(1142596565425439559)
XLA Ops:
  6.5 1.6 fusion.51
  8.1 4.8 %collective-permute-start = (bf16[3,64,1,256]{3,1,2,0:T(8,128)(2,1)S(1)}, bf16[3,64,1,256]{3,1,2,0:T(8,128)(2,1)S(1)}, u32[]{:S(2)}, u32[]{:S(2)}) collective-permute-start(bf16[3,64,1,256]{3,1,2,0:T(8,128)(2,1)S(1)} %copy.36), channel_id=1, source_target_pairs={{0,16},{1,17},{2,18},{3,19},{4,20},{5,21},{6,22},{7,23},{8,24},{9,... | collective-permute-start | bytes 294920 | tf_op jit(solution)/shard_map/ppermute | solution.py:14
  13.0 1.3 collective-permute-start.1
  14.3 0.9 collective-permute-done
  15.2 4.3 %collective-permute-done.1 = bf16[3,64,1,256]{3,1,2,0:T(8,128)(2,1)S(1)} collective-permute-done((bf16[3,64,1,256]{3,1,2,0:T(8,128)(2,1)S(1)}, bf16[3,64,1,256]{3,1,2,0:T(8,128)(2,1)S(1)}, u32[]{:S(2)}, u32[]{:S(2)}) %collective-permute-start.1) | collective-permute-done | bytes 98336 | tf_op jit(solution)/shard_map/ppermute | solution.py:15
  19.7 1.3 collective-permute-start.2
  21.0 1.3 collective-permute-start.3
  22.3 3.9 %collective-permute-done.3 = bf16[3,64,6,1]{3,1,2,0:T(8,128)(2,1)S(1)} collective-permute-done((bf16[3,64,6,1]{3,1,2,0:T(8,128)(2,1)S(1)}, bf16[3,64,6,1]{3,1,2,0:T(8,128)(2,1)S(1)}, u32[]{:S(2)}, u32[]{:S(2)}) %collective-permute-start.3) | collective-permute-done | bytes 2336 | tf_op jit(solution)/shard_map/ppermute | solution.py:15
  27.9 1.2 convolution_bitcast_fusion
  29.1 0.8 copy.29
  29.9 27.3 %psum.21 = f32[64,64]{1,0:T(8,128)S(1)} all-reduce(f32[64,64]{1,0:T(8,128)S(1)} %convolution_bitcast_fusion), channel_id=1, replica_groups=mesh['sx'=2,'sy'=4,'ta'=4] {'sx','sy'}, use_global_device_ids=true, to_apply=%region_0.0 | all-reduce | flops 4096 | bytes 32768 | tf_op jit(solution)/shard_map/psum | solution.py:92
  57.2 0.7 fusion.39
  58.4 5.8 %cholesky.59 = f32[64,64]{1,0:T(8,128)S(1)} custom-call(f32[64,64]{1,0:T(8,128)S(1)} %fusion.34), custom_call_target="Cholesky" | custom-call | tf_op jit(solution)/shard_map/jit(cholesky)/cholesky | solution.py:33
  64.9 0.7 fusion.18
  65.6 4.9 %custom-call.9 = f32[1,64,64]{1,2,0:T(8,128)S(1)} custom-call(f32[1,64,64]{2,1,0:T(8,128)S(1)} %fusion.18), custom_call_target="InvertDiagBlocksLowerTriangular" | custom-call | tf_op jit(solution)/shard_map/jit(_solve_triangular)/triangular_solve | solution.py:34
  71.3 0.7 reshape.31
  72.1 1.2 fusion.52
  73.4 1.6 collective-permute-start.4
  75.1 26.4 %collective-permute-done.4 = f32[64,5120]{1,0:T(8,128)} collective-permute-done((f32[64,5120]{1,0:T(8,128)S(1)}, f32[64,5120]{1,0:T(8,128)}, u32[]{:S(2)}, u32[]{:S(2)}) %collective-permute-start.4) | collective-permute-done | bytes 1310752 | tf_op jit(solution)/shard_map/ppermute | solution.py:21
  101.5 1.9 broadcast_select_fusion.1
  103.4 1.2 fusion.53
  104.6 1.2 fusion.54
  105.8 1.2 fusion.55
  107.1 0.7 maximum_maximum_fusion
  108.1 53.6 %all-reduce.3.cloned.1.call-done = f32[128,128]{1,0:T(8,128)} async-done(((f32[128,128]{1,0:T(8,128)}), f32[128,128]{1,0:T(8,128)}) %all-reduce.3.cloned.1.call-update) | async-done | bytes 65552 | tf_op jit(solution)/shard_map/psum | solution.py:111
  161.7 1.1 fusion.45
  163.1 5.8 %cholesky.70 = f32[64,64]{1,0:T(8,128)S(1)} custom-call(f32[64,64]{1,0:T(8,128)S(1)} %fusion.32), custom_call_target="Cholesky" | custom-call | tf_op jit(solution)/shard_map/jit(cholesky)/cholesky | solution.py:33
  169.6 0.7 fusion.19
  170.3 4.9 %custom-call.11 = f32[1,64,64]{1,2,0:T(8,128)S(1)} custom-call(f32[1,64,64]{2,1,0:T(8,128)S(1)} %fusion.19), custom_call_target="InvertDiagBlocksLowerTriangular" | custom-call | tf_op jit(solution)/shard_map/jit(_solve_triangular)/triangular_solve | solution.py:34
  175.2 1.5 select_reduce_fusion.1
  177.6 1.3 fusion.24
  178.9 1.2 convolution_add_fusion.1
  180.1 2.5 collective-permute-start.5
  182.6 56.5 %collective-permute-done.5 = f32[64,5120]{1,0:T(8,128)} collective-permute-done((f32[64,5120]{1,0:T(8,128)S(1)}, f32[64,5120]{1,0:T(8,128)}, u32[]{:S(2)}, u32[]{:S(2)}) %collective-permute-start.5) | collective-permute-done | bytes 1310752 | tf_op jit(solution)/shard_map/ppermute | solution.py:21
  239.1 1.9 broadcast_select_fusion.3
  241.0 1.2 fusion.56
  242.2 1.2 fusion.57
  243.4 1.2 fusion.58
  244.7 0.7 maximum_maximum_fusion.1
  245.4 52.0 %all-reduce.5.cloned.1.call-done = f32[128,128]{1,0:T(8,128)} async-done(((f32[128,128]{1,0:T(8,128)}), f32[128,128]{1,0:T(8,128)}) %all-reduce.5.cloned.1.call-update) | async-done | bytes 65552 | tf_op jit(solution)/shard_map/psum | solution.py:111
  297.4 1.1 fusion.43
  298.8 5.8 %cholesky.81 = f32[64,64]{1,0:T(8,128)S(1)} custom-call(f32[64,64]{1,0:T(8,128)S(1)} %fusion.29), custom_call_target="Cholesky" | custom-call | tf_op jit(solution)/shard_map/jit(cholesky)/cholesky | solution.py:33
  305.3 0.7 fusion.20
  306.0 4.9 %custom-call.12 = f32[1,64,64]{1,2,0:T(8,128)S(1)} custom-call(f32[1,64,64]{2,1,0:T(8,128)S(1)} %fusion.20), custom_call_target="InvertDiagBlocksLowerTriangular" | custom-call | tf_op jit(solution)/shard_map/jit(_solve_triangular)/triangular_solve | solution.py:34
  310.9 1.5 select_reduce_fusion
  313.3 1.3 fusion.21
  314.5 1.3 convolution_add_fusion
  316.4 1.2 constant_dynamic-slice_fusion
  (54 shorter events, 6.7 us)
Async XLA Ops:
  6.5 8.7 %copy-start.2 = (bf16[3,64,4,256]{3,2,1,0:T(4,128)(2,1)S(1)}, bf16[3,64,4,256]{3,2,1,0:T(4,128)(2,1)}, u32[]{:S(2)}) copy-start(bf16[3,64,4,256]{3,2,1,0:T(4,128)(2,1)} %param.6) | copy-start | bytes 1179652
  6.5 155.2 %all-reduce.3.cloned.1.call-start = ((), (), s32[]{:S(2)}) async-start(), calls=%async_computation | async-start | bytes 131072 | tf_op jit(solution)/shard_map/psum | solution.py:111
  8.1 7.0 %collective-permute-start = (bf16[3,64,1,256]{3,1,2,0:T(8,128)(2,1)S(1)}, bf16[3,64,1,256]{3,1,2,0:T(8,128)(2,1)S(1)}, u32[]{:S(2)}, u32[]{:S(2)}) collective-permute-start(bf16[3,64,1,256]{3,1,2,0:T(8,128)(2,1)S(1)} %copy.36), channel_id=1, source_target_pairs={{0,16},{1,17},{2,18},{3,19},{4,20},{5,21},{6,22},{7,23},{8,24},{9,... | collective-permute-start | bytes 294920 | tf_op jit(solution)/shard_map/ppermute | solution.py:14
  13.0 6.5 %collective-permute-start.1 = (bf16[3,64,1,256]{3,1,2,0:T(8,128)(2,1)S(1)}, bf16[3,64,1,256]{3,1,2,0:T(8,128)(2,1)S(1)}, u32[]{:S(2)}, u32[]{:S(2)}) collective-permute-start(bf16[3,64,1,256]{3,1,2,0:T(8,128)(2,1)S(1)} %copy.37), channel_id=1, source_target_pairs={{16,0},{17,1},{18,2},{19,3},{20,4},{21,5},{22,6},{23,7},{24,8},{25... | collective-permute-start | bytes 294920 | tf_op jit(solution)/shard_map/ppermute | solution.py:15
  19.7 2.6 collective-permute-start.2
  21.0 5.2 %collective-permute-start.3 = (bf16[3,64,6,1]{3,1,2,0:T(8,128)(2,1)S(1)}, bf16[3,64,6,1]{3,1,2,0:T(8,128)(2,1)S(1)}, u32[]{:S(2)}, u32[]{:S(2)}) collective-permute-start(bf16[3,64,6,1]{3,1,2,0:T(8,128)(2,1)S(1)} %get-tuple-element.15), channel_id=1, source_target_pairs={{4,0},{8,4},{12,8},{5,1},{9,5},{13,9},{6,2},{10,6},{14,10},{7,3},{... | collective-permute-start | bytes 6920 | tf_op jit(solution)/shard_map/ppermute | solution.py:15
  29.1 28.9 %copy-start.3 = (s32[64,64]{1,0:T(8,128)S(1)}, s32[64,64]{1,0:T(8,128)}, u32[]{:S(2)}) copy-start(s32[64,64]{1,0:T(8,128)} %param.7) | copy-start | bytes 49156
  73.4 1.7 copy-start.1
  73.4 28.1 %collective-permute-start.4 = (f32[64,5120]{1,0:T(8,128)S(1)}, f32[64,5120]{1,0:T(8,128)}, u32[]{:S(2)}, u32[]{:S(2)}) collective-permute-start(f32[64,5120]{1,0:T(8,128)S(1)} %fusion.52), channel_id=1, source_target_pairs={{0,1},{1,0},{2,3},{3,2},{4,5},{5,4},{6,7},{7,6},{8,9},{9,8},{10,11... | collective-permute-start | bytes 3932168 | tf_op jit(solution)/shard_map/ppermute | solution.py:21
  105.8 2.3 copy-start.4
  107.8 189.6 %all-reduce.5.cloned.1.call-start = ((), (), s32[]{:S(2)}) async-start(), calls=%async_computation.1 | async-start | bytes 131072 | tf_op jit(solution)/shard_map/psum | solution.py:111
  180.1 2.5 copy-start
  180.1 59.0 %collective-permute-start.5 = (f32[64,5120]{1,0:T(8,128)S(1)}, f32[64,5120]{1,0:T(8,128)}, u32[]{:S(2)}, u32[]{:S(2)}) collective-permute-start(f32[64,5120]{1,0:T(8,128)S(1)} %convolution_add_fusion.1), channel_id=1, source_target_pairs={{0,2},{1,3},{2,0},{3,1},{4,6},{5,7},{6,4},{7,5},{8,10},{9,11},{10,... | collective-permute-start | bytes 3932168 | tf_op jit(solution)/shard_map/ppermute | solution.py:21
Sparse Core Ops, SparseCore 0:
  107.9 53.7 all-reduce.2
  245.5 51.8 all-reduce.4
where the time goes:
time: 325 us
  waiting for transfers between devices  198 us (61%)
  other arithmetic  46.7 us (14%)
  blocking collectives  27.3 us (8%)
  matrix products  18 us (6%)
  between operations  16 us (5%)
  starting transfers between devices  13.1 us (4%)
  local copies, waits for them, and re-layouts  5.83 us (2%)
    psum x2, waiting for transfers between devices, local(): pair_total = lax.psum(local_pair, ('sx', 'sy'))  106 us
    ppermute x2, waiting for transfers between devices, from_partner(): lax.ppermute(x, axis, [(i, i ^ 1 << apart) for i in range(lax.axis_size(a...  82.9 us
    psum x1, blocking collectives, local(): gram_mat = lax.psum(matmul_hi(strain, strain.T), ('sx', 'sy'))  27.3 us
    another operation x9, other arithmetic, coefficients(): factor = jnp.linalg.cholesky(reduced)  19.6 us
    dot_general x18, matrix products, matmul_hi(): return jnp.dot(left, right, precision=lax.Precision.HIGHEST)  17.4 us
    another operation x6, other arithmetic, coefficients(): solved = jax.scipy.linalg.solve_triangular(factor, imaged.T, lower=True)  16.6 us
    ppermute x2, waiting for transfers between devices, padded_2(): after = lax.ppermute(leading, axis, down)  8.18 us
  transfers between devices with their start and end apart: 8, of which 7 were waited for; matrix products, arithmetic and copies ran while one was open for 0% of the time, Pallas kernels for 0%

commit v1 on v0

v1 whole, which is shorter than its diff:
```python
import jax
import jax.numpy as jnp
from jax import lax
from jax.experimental import pallas as pl
from jax.experimental.pallas import tpu as pltpu
from jax.sharding import PartitionSpec as P

HI = lax.Precision.HIGHEST


def mm(left, right, contract=(1, 0)):
    return lax.dot_general(
        left,
        right,
        (((contract[0],), (contract[1],)), ((), ())),
        precision=HI,
        preferred_element_type=jnp.float32,
    )


def eye(rows, cols):
    return (
        lax.broadcasted_iota(jnp.int32, (rows, cols), 0)
        == lax.broadcasted_iota(jnp.int32, (rows, cols), 1)
    ).astype(jnp.float32)


def inverse_factors(mats):
    n = mats[0].shape[0]
    batch = len(mats)
    tiles = n // 8
    ident = eye(n, n)
    width = 2 * n
    work = [
        [jnp.concatenate([m, ident], axis=1)[8 * i : 8 * i + 8] for i in range(tiles)]
        for m in mats
    ]
    sub = lax.broadcasted_iota(jnp.int32, (8, width), 0)
    done = [[None] * tiles for _ in range(batch)]
    for p in range(tiles):
        cols = [
            [
                [
                    jnp.broadcast_to(work[b][i][:, 8 * p + k : 8 * p + k + 1], (8, width))
                    for i in range(p, tiles)
                ]
                for k in range(8)
            ]
            for b in range(batch)
        ]
        for b in range(batch):
            head = work[b][p]
            rest = [work[b][i] for i in range(p + 1, tiles)]
            scales = jnp.zeros((8, width), jnp.float32)
            for k in range(8):
                pivot = cols[b][k][0][k : k + 1]
                inv = 1.0 / pivot
                scales = jnp.where(sub == k, jnp.broadcast_to(inv, (8, width)), scales)
                row = head[k : k + 1] * inv
                across = [cols[b][j][0][k : k + 1] * inv for j in range(k + 1, 8)]
                below = jnp.where(sub > k, cols[b][k][0], 0.0)
                head = head - below * row
                for j in range(k + 1, 8):
                    cols[b][j][0] = cols[b][j][0] - below * across[j - k - 1]
                for i in range(1, tiles - p):
                    factor = cols[b][k][i]
                    rest[i - 1] = rest[i - 1] - factor * row
                    for j in range(k + 1, 8):
                        cols[b][j][i] = cols[b][j][i] - factor * across[j - k - 1]
            done[b][p] = head * jnp.sqrt(scales)
            for i in range(p + 1, tiles):
                work[b][i] = rest[i - p - 1]
    return [jnp.concatenate(done[b], axis=0)[:, n:] for b in range(batch)]


def solve_steps(grams, rotation):
    order_n = rotation.shape[0]
    ident = eye(order_n, order_n)
    imaged = [mm(g, rotation) for g in grams]
    reduced = [mm(rotation, z, (0, 0)) for z in imaged]
    inverses = inverse_factors(reduced)
    out = []
    for g, z, inverse in zip(grams, imaged, inverses):
        trace = jnp.sum(jnp.sum(g * ident, axis=0, keepdims=True), axis=1, keepdims=True)
        out.append(mm(inverse, z, (1, 1)) * lax.rsqrt(trace / order_n))
    return out


def block_diagonal(low, high):
    zero_low = jnp.zeros((low.shape[0], high.shape[1]), jnp.float32)
    zero_high = jnp.zeros((high.shape[0], low.shape[1]), jnp.float32)
    return jnp.concatenate(
        [
            jnp.concatenate([low, zero_low], axis=1),
            jnp.concatenate([zero_high, high], axis=1),
        ],
        axis=0,
    )


def tree_kernel(gram_ref, strain_ref, first_ref, merge_ref, out_ref):
    width = first_ref.shape[0]
    num_levels = merge_ref.shape[0]
    blocks = gram_ref.shape[0] // width
    first = eye(width, width) + first_ref[...].astype(jnp.float32) * (0.5 / 512.0)
    span = width
    coefs = solve_steps(
        [gram_ref[b * span : (b + 1) * span, b * span : (b + 1) * span] for b in range(blocks)],
        first,
    )
    stacked = jnp.concatenate([eye(width, width)] * 2, axis=0) * (2.0**-0.5)
    for level in range(num_levels):
        rotation = stacked + merge_ref[level].astype(jnp.float32) * (0.5 / (64.0 * 128.0**0.5))
        span *= 2
        pairs = [block_diagonal(coefs[2 * i], coefs[2 * i + 1]) for i in range(len(coefs) // 2)]
        grams = []
        for i, pair in enumerate(pairs):
            part = gram_ref[i * span : (i + 1) * span, i * span : (i + 1) * span]
            grams.append(mm(mm(pair, part), pair, (1, 1)))
        solved = solve_steps(grams, rotation)
        coefs = [mm(kt, pair) for kt, pair in zip(solved, pairs)]
    out_ref[...] = mm(coefs[0], strain_ref[...])


def padded_2(x, sides, width):
    for axis, dim in sides:
        size, length = (lax.axis_size(axis), x.shape[dim])
        up = [(i, (i + 1) % size) for i in range(size - 1)]
        down = [(j, i) for i, j in up]
        last = lax.slice_in_dim(x, length - width, length, axis=dim)
        leading = lax.slice_in_dim(x, 0, width, axis=dim)
        before = lax.ppermute(last, axis, up)
        after = lax.ppermute(leading, axis, down)
        x = jnp.concatenate([before, x, after], axis=dim)
    return x


def diff_x(field):
    return 0.5 * (field[:, 2:, 1:-1] - field[:, :-2, 1:-1])


def diff_y(field):
    return 0.5 * (field[:, 1:-1, 2:] - field[:, 1:-1, :-2])


def strain_rows(padded):
    comp_u = padded[0]
    comp_v = padded[1]
    comp_w = padded[2]
    fields = jnp.stack(
        [
            diff_x(comp_u),
            diff_y(comp_v),
            0.5 * (diff_y(comp_u) + diff_x(comp_v)),
            0.5 * diff_x(comp_w),
            0.5 * diff_y(comp_w),
        ],
        axis=1,
    )
    return fields.reshape(fields.shape[0], -1)


def local(velocity, seeds_first, seeds_merge):
    width = seeds_first.shape[0]
    cells_x = velocity.shape[2]
    cells_y = velocity.shape[3]
    blocks = lax.axis_size("ta")
    quarter = cells_y // blocks
    rimmed = padded_2(velocity, (("sx", 2), ("sy", 3)), 1)
    pieces = jnp.stack(
        [rimmed[..., i * quarter : (i + 1) * quarter + 2] for i in range(blocks)], axis=0
    )
    pieces = lax.all_to_all(pieces, "ta", 0, 0, tiled=True)
    pieces = pieces.transpose(1, 0, 2, 3, 4).reshape(
        3, blocks * width, cells_x + 2, quarter + 2
    )
    strain = strain_rows(pieces.astype(jnp.float32))
    gram = lax.psum(jnp.dot(strain, strain.T, precision=HI), ("sx", "sy", "ta"))
    vmem = pl.BlockSpec(memory_space=pltpu.VMEM)
    out = pl.pallas_call(
        tree_kernel,
        out_shape=jax.ShapeDtypeStruct((width, strain.shape[1]), jnp.float32),
        in_specs=[vmem] * 4,
        out_specs=vmem,
        compiler_params=pltpu.CompilerParams(vmem_limit_bytes=32 * 2**20),
        name="tree",
    )(gram, strain, seeds_first, seeds_merge)
    return out.reshape(width, 5, cells_x, quarter)


def solution(mesh):
    in_specs = (P(None, "ta", "sx", "sy"), P(), P())
    out_specs = P(None, None, "sx", ("sy", "ta"))
    return jax.shard_map(local, mesh=mesh, in_specs=in_specs, out_specs=out_specs, check_vma=False)
```

time: 325 us -> 213 us (0.66)
  waiting for transfers between devices: 198 us -> 132 us
  other arithmetic: 46.7 us -> 1.38 us
  matrix products: 18 us -> 2.95 us
  Pallas kernels: 0 us -> 10.4 us
  blocking collectives: 27.3 us -> 32.6 us
  local copies, waits for them, and re-layouts: 5.83 us -> 10.4 us
  starting transfers between devices: 13.1 us -> 8.74 us
    ppermute x2 -> x0, waiting for transfers between devices: 82.9 us -> none  [from_partner(): lax.ppermute(x, axis, [(i, i ^ 1 << apart) for i in range(lax.axis_size(a...]
    another operation x15 -> x2, other arithmetic: 36.2 us -> 0.84 us  [local(): jnp.stack([rimmed[..., i * quarter:(i + 1) * quarter + 2] for i in range(...]
    all_to_all x0 -> x1, blocking collectives: none -> 32.6 us  [local(): pieces = lax.all_to_all(pieces, 'ta', 0, 0, tiled=True)]
    psum x1 -> x0, blocking collectives: 27.3 us -> none  [local(): gram_mat = lax.psum(matmul_hi(strain, strain.T), ('sx', 'sy'))]
    psum x2 -> x1, waiting for transfers between devices: 106 us -> 123 us  [local(): gram = lax.psum(jnp.dot(strain, strain.T, precision=HI), ('sx', 'sy', 'ta'))]
    dot_general x18 -> x1, matrix products: 17.4 us -> 2.95 us  [local(): gram = lax.psum(jnp.dot(strain, strain.T, precision=HI), ('sx', 'sy', 'ta'))]
    pallas_call x0 -> x1, Pallas kernels: none -> 10.4 us  [local(): pl.pallas_call(tree_kernel, out_shape=jax.ShapeDtypeStruct((width, strain...]
    ppermute x2 -> x0, starting transfers between devices: 4.11 us -> none  [from_partner(): lax.ppermute(x, axis, [(i, i ^ 1 << apart) for i in range(lax.axis_size(a...]
  transfers between devices with their start and end apart: 8 -> 5, of which waited for: 7 -> 4; matrix products, arithmetic and copies ran while one was open for 0% -> 0% of each run, Pallas kernels for 0% -> 0%
where the time goes in v1:
time: 213 us; the launch traced here: 212 us
  waiting for transfers between devices  132 us (62%)
  blocking collectives  32.6 us (15%)
  between operations  13.6 us (6%)
  local copies, waits for them, and re-layouts  10.4 us (5%)
  Pallas kernels  10.4 us (5%)
  starting transfers between devices  8.74 us (4%)
  matrix products  2.95 us (1%)
    psum x1, waiting for transfers between devices, local(): gram = lax.psum(jnp.dot(strain, strain.T, precision=HI), ('sx', 'sy', 'ta'))  123 us
    all_to_all x1, blocking collectives, local(): pieces = lax.all_to_all(pieces, 'ta', 0, 0, tiled=True)  32.6 us
    pallas_call x1, Pallas kernels, local(): pl.pallas_call(tree_kernel, out_shape=jax.ShapeDtypeStruct((width, strain...  10.4 us
    ppermute x2, waiting for transfers between devices, padded_2(): after = lax.ppermute(leading, axis, down)  8.18 us
    ppermute x2, starting transfers between devices, padded_2(): before = lax.ppermute(last, axis, up)  6.16 us
  transfers between devices with their start and end apart: 5, of which 4 were waited for; matrix products, arithmetic and copies ran while one was open for 0% of the time, Pallas kernels for 0%

profile of v1, /device:TPU:0, one launch (start us, length us, event | category | flops | bytes accessed | tf_op | source)
XLA Modules:
  0.0 212.4 jit_solution(15993277122225678396)
XLA Ops:
  6.5 0.0 copy-start.3
  6.5 0.0 all-reduce.2.cloned.1.call-start
  6.5 1.5 fusion.20
  8.1 4.8 %collective-permute-start = (bf16[3,64,1,256]{3,1,2,0:T(8,128)(2,1)S(1)}, bf16[3,64,1,256]{3,1,2,0:T(8,128)(2,1)S(1)}, u32[]{:S(2)}, u32[]{:S(2)}) collective-permute-start(bf16[3,64,1,256]{3,1,2,0:T(8,128)(2,1)S(1)} %copy.24), channel_id=1, source_target_pairs={{0,16},{1,17},{2,18},{3,19},{4,20},{5,21},{6,22},{7,23},{8,24},{9,... | collective-permute-start | bytes 294920 | tf_op jit(solution)/shard_map/ppermute | solution.py:132
  13.0 1.3 collective-permute-start.1
  14.3 0.9 collective-permute-done
  15.1 0.0 copy-done.3
  15.2 4.3 %collective-permute-done.1 = bf16[3,64,1,256]{3,1,2,0:T(8,128)(2,1)S(1)} collective-permute-done((bf16[3,64,1,256]{3,1,2,0:T(8,128)(2,1)S(1)}, bf16[3,64,1,256]{3,1,2,0:T(8,128)(2,1)S(1)}, u32[]{:S(2)}, u32[]{:S(2)}) %collective-permute-start.1) | collective-permute-done | bytes 98336 | tf_op jit(solution)/shard_map/ppermute | solution.py:133
  19.5 0.2 fusion.19
  19.6 1.3 collective-permute-start.2
  21.0 1.3 collective-permute-start.3
  22.3 0.0 collective-permute-done.2
  22.3 3.9 %collective-permute-done.3 = bf16[3,64,6,1]{3,1,2,0:T(8,128)(2,1)S(1)} collective-permute-done((bf16[3,64,6,1]{3,1,2,0:T(8,128)(2,1)S(1)}, bf16[3,64,6,1]{3,1,2,0:T(8,128)(2,1)S(1)}, u32[]{:S(2)}, u32[]{:S(2)}) %collective-permute-start.3) | collective-permute-done | bytes 2336 | tf_op jit(solution)/shard_map/ppermute | solution.py:133
  26.2 0.5 fusion.1
  26.7 0.3 pad_maximum_fusion
  27.0 32.6 %all_to_all.5 = bf16[4,3,64,6,66]{4,2,3,1,0:T(8,128)(2,1)S(1)} all-to-all(bf16[4,3,64,6,66]{4,2,3,1,0:T(8,128)(2,1)S(1)} %pad_maximum_fusion), channel_id=1, replica_groups=mesh['sx'=2,'sy'=4,'ta'=4] {'ta'}, dimensions={0} | all-to-all | bytes 1216512 | tf_op jit(solution)/shard_map/all_to_all | solution.py:173
  59.6 0.3 convert_bitcast_fusion
  59.9 1.3 fusion.18
  61.3 0.4 copy.17
  61.7 0.5 squeeze.9
  62.2 1.5 copy.18
  63.7 0.5 squeeze.10
  64.2 0.0 copy-start.2
  64.3 0.1 fusion.11
  64.4 1.0 copy-done.2
  65.4 0.4 copy.19
  65.7 0.5 squeeze.11
  66.3 0.0 copy-start.4
  66.3 3.0 %convolution_bitcast_fusion = f32[256,256]{1,0:T(8,128)} fusion(f32[256,5,4,64]{0,3,2,1:T(8,128)S(1)} %fusion.4), kind=kOutput, calls=%fused_computation.2 | convolution fusion | flops 1006632960 | bytes 1572864 | tf_op jit(solution)/shard_map/dot_general | solution.py:178
  69.3 0.0 all-reduce.2.cloned.1.call-update
  69.3 0.0 copy-done.4
  69.3 0.1 copy.21.merge_ref
  69.4 0.0 copy-start.1
  69.5 0.4 copy.20.strain_ref
  69.9 123.2 %all-reduce.2.cloned.1.call-done.gram_ref = f32[256,256]{1,0:T(8,128)} async-done(((f32[256,256]{1,0:T(8,128)}), f32[256,256]{1,0:T(8,128)}) %all-reduce.2.cloned.1.call-update) | async-done | bytes 262160 | tf_op jit(solution)/shard_map/psum | solution.py:178
  193.0 0.0 copy-done.1
  193.0 0.0 copy-start
  193.0 0.9 copy-done
  194.0 10.4 %tree.1 = f32[64,1280]{1,0:T(8,128)S(1)} custom-call(f32[256,256]{1,0:T(8,128)S(1)} %copy-done, f32[256,1280]{1,0:T(8,128)S(1)} %copy.20.strain_ref, s32[64,64]{1,0:T(8,128)S(1)} %copy-done.1, s32[2,128,64]{2,1,0:T(8,128)S(1)} %copy.21.merge_ref), custom_call_target="tpu_custom_call" | custom-call | tf_op jit(solution)/shard_map/tree/pallas_call | solution.py:180
  204.4 1.1 reshape.15
  (9 shorter events, 0.3 us)
Async XLA Ops:
  6.5 8.6 %copy-start.3 = (bf16[3,64,4,256]{3,2,1,0:T(4,128)(2,1)S(1)}, bf16[3,64,4,256]{3,2,1,0:T(4,128)(2,1)}, u32[]{:S(2)}) copy-start(bf16[3,64,4,256]{3,2,1,0:T(4,128)(2,1)} %param.3) | copy-start | bytes 1179652
  6.5 186.5 %all-reduce.2.cloned.1.call-start = ((), (), s32[]{:S(2)}) async-start(), calls=%async_computation.1 | async-start | bytes 524288 | tf_op jit(solution)/shard_map/psum | solution.py:178
  8.1 7.0 %collective-permute-start = (bf16[3,64,1,256]{3,1,2,0:T(8,128)(2,1)S(1)}, bf16[3,64,1,256]{3,1,2,0:T(8,128)(2,1)S(1)}, u32[]{:S(2)}, u32[]{:S(2)}) collective-permute-start(bf16[3,64,1,256]{3,1,2,0:T(8,128)(2,1)S(1)} %copy.24), channel_id=1, source_target_pairs={{0,16},{1,17},{2,18},{3,19},{4,20},{5,21},{6,22},{7,23},{8,24},{9,... | collective-permute-start | bytes 294920 | tf_op jit(solution)/shard_map/ppermute | solution.py:132
  13.0 6.5 %collective-permute-start.1 = (bf16[3,64,1,256]{3,1,2,0:T(8,128)(2,1)S(1)}, bf16[3,64,1,256]{3,1,2,0:T(8,128)(2,1)S(1)}, u32[]{:S(2)}, u32[]{:S(2)}) collective-permute-start(bf16[3,64,1,256]{3,1,2,0:T(8,128)(2,1)S(1)} %copy.25), channel_id=1, source_target_pairs={{16,0},{17,1},{18,2},{19,3},{20,4},{21,5},{22,6},{23,7},{24,8},{25... | collective-permute-start | bytes 294920 | tf_op jit(solution)/shard_map/ppermute | solution.py:133
  19.6 2.6 %collective-permute-start.2 = (bf16[3,64,6,1]{3,1,2,0:T(8,128)(2,1)S(1)}, bf16[3,64,6,1]{3,1,2,0:T(8,128)(2,1)S(1)}, u32[]{:S(2)}, u32[]{:S(2)}) collective-permute-start(bf16[3,64,6,1]{3,1,2,0:T(8,128)(2,1)S(1)} %get-tuple-element.12), channel_id=1, source_target_pairs={{0,4},{4,8},{8,12},{1,5},{5,9},{9,13},{2,6},{6,10},{10,14},{3,7},{... | collective-permute-start | bytes 6920 | tf_op jit(solution)/shard_map/ppermute | solution.py:132
  21.0 5.2 %collective-permute-start.3 = (bf16[3,64,6,1]{3,1,2,0:T(8,128)(2,1)S(1)}, bf16[3,64,6,1]{3,1,2,0:T(8,128)(2,1)S(1)}, u32[]{:S(2)}, u32[]{:S(2)}) collective-permute-start(bf16[3,64,6,1]{3,1,2,0:T(8,128)(2,1)S(1)} %get-tuple-element.13), channel_id=1, source_target_pairs={{4,0},{8,4},{12,8},{5,1},{9,5},{13,9},{6,2},{10,6},{14,10},{7,3},{... | collective-permute-start | bytes 6920 | tf_op jit(solution)/shard_map/ppermute | solution.py:133
  64.2 1.1 copy-start.2
  66.3 3.0 %copy-start.4 = (s32[2,128,64]{1,2,0:T(8,128)S(1)}, s32[2,128,64]{1,2,0:T(8,128)}, u32[]{:S(2)}) copy-start(s32[2,128,64]{1,2,0:T(8,128)} %param.5) | copy-start | bytes 196612
  69.4 123.6 %copy-start.1 = (s32[64,64]{1,0:T(8,128)S(1)}, s32[64,64]{1,0:T(8,128)}, u32[]{:S(2)}) copy-start(s32[64,64]{1,0:T(8,128)} %first_ref.1) | copy-start | bytes 49156
  193.0 1.0 copy-start
Sparse Core Ops, SparseCore 0:
  69.4 123.5 all-reduce.1

commit v2 on v1

--- a/solution.py
+++ b/solution.py
@@ -1,3 +1,5 @@
+import functools
+
 import jax
 import jax.numpy as jnp
 from jax import lax
@@ -100,86 +102,379 @@
 
 def tree_kernel(gram_ref, strain_ref, first_ref, merge_ref, out_ref):
     width = first_ref.shape[0]
-    num_levels = merge_ref.shape[0]
-    blocks = gram_ref.shape[0] // width
+    pair = 2 * width
+    gram_low = gram_ref[:pair]
+    gram_cross = gram_ref[pair : 2 * pair]
+    gram_high = gram_ref[2 * pair : 3 * pair]
     first = eye(width, width) + first_ref[...].astype(jnp.float32) * (0.5 / 512.0)
-    span = width
+    stacked = jnp.concatenate([eye(width, width)] * 2, axis=0) * (2.0**-0.5)
+    turns = [
+        stacked + merge_ref[level].astype(jnp.float32) * (0.5 / (64.0 * 128.0**0.5))
+        for level in range(2)
+    ]
     coefs = solve_steps(
-        [gram_ref[b * span : (b + 1) * span, b * span : (b + 1) * span] for b in range(blocks)],
+        [g[i * width : (i + 1) * width, i * width : (i + 1) * width] for g in (gram_low, gram_high) for i in (0, 1)],
         first,
     )
-    stacked = jnp.concatenate([eye(width, width)] * 2, axis=0) * (2.0**-0.5)
-    for level in range(num_levels):
-        rotation = stacked + merge_ref[level].astype(jnp.float32) * (0.5 / (64.0 * 128.0**0.5))
-        span *= 2
-        pairs = [block_diagonal(coefs[2 * i], coefs[2 * i + 1]) for i in range(len(coefs) // 2)]
-        grams = []
-        for i, pair in enumerate(pairs):
-            part = gram_ref[i * span : (i + 1) * span, i * span : (i + 1) * span]
-            grams.append(mm(mm(pair, part), pair, (1, 1)))
-        solved = solve_steps(grams, rotation)
-        coefs = [mm(kt, pair) for kt, pair in zip(solved, pairs)]
-    out_ref[...] = mm(coefs[0], strain_ref[...])
-
-
-def padded_2(x, sides, width):
-    for axis, dim in sides:
-        size, length = (lax.axis_size(axis), x.shape[dim])
-        up = [(i, (i + 1) % size) for i in range(size - 1)]
-        down = [(j, i) for i, j in up]
-        last = lax.slice_in_dim(x, length - width, length, axis=dim)
-        leading = lax.slice_in_dim(x, 0, width, axis=dim)
-        before = lax.ppermute(last, axis, up)
-        after = lax.ppermute(leading, axis, down)
-        x = jnp.concatenate([before, x, after], axis=dim)
-    return x
-
-
-def diff_x(field):
-    return 0.5 * (field[:, 2:, 1:-1] - field[:, :-2, 1:-1])
-
-
-def diff_y(field):
-    return 0.5 * (field[:, 1:-1, 2:] - field[:, 1:-1, :-2])
-
-
-def strain_rows(padded):
-    comp_u = padded[0]
-    comp_v = padded[1]
-    comp_w = padded[2]
-    fields = jnp.stack(
+    low, high = block_diagonal(coefs[0], coefs[1]), block_diagonal(coefs[2], coefs[3])
+    solved = solve_steps(
+        [mm(mm(low, gram_low), low, (1, 1)), mm(mm(high, gram_high), high, (1, 1))], turns[0]
+    )
+    low, high = mm(solved[0], low), mm(solved[1], high)
+    cross = mm(mm(high, gram_cross), low, (1, 1))
+    top = jnp.concatenate([mm(mm(low, gram_low), low, (1, 1)), cross.T], axis=1)
+    bottom = jnp.concatenate([cross, mm(mm(high, gram_high), high, (1, 1))], axis=1)
+    last = solve_steps([jnp.concatenate([top, bottom], axis=0)], turns[1])[0]
+    weights = jnp.concatenate([mm(last[:, :width], low), mm(last[:, width:], high)], axis=1)
+    out_ref[...] = mm(weights, strain_ref[...])
+
+
+MESH = pl.DeviceIdType.MESH
+
+
+def loop(start, stop, body):
+    if stop - start <= 8:
+        for i in range(start, stop):
+            body(i)
+    else:
+        lax.fori_loop(start, stop, lambda i, carry: (body(i), carry)[1], 0)
+
+
+def dot16(left, right, contract=(1, 0)):
+    return lax.dot_general(
+        left,
+        right,
+        (((contract[0],), (contract[1],)), ((), ())),
+        preferred_element_type=jnp.float32,
+    )
+
+
+def iotas(rows, cols):
+    return (
+        lax.broadcasted_iota(jnp.int32, (rows, cols), 0),
+        lax.broadcasted_iota(jnp.int32, (rows, cols), 1),
+    )
+
+
+def signed_half(plus, minus):
+    return (0.5 * plus.astype(jnp.float32) - 0.5 * minus.astype(jnp.float32)).astype(jnp.bfloat16)
+
+
+def gather_kernel(
+    quarter, nx, ny, nt,
+    chunk_ref, strain_ref, gram_ref,
+    held, from_up, from_down, edges, from_left, from_right, parts, landed, slices, whole,
+    chunk_sems, x_sems, y_sems, rim_sems, scatter_sems, line_sems, spread_sems,
+):
+    ix, iy, it = lax.axis_index("sx"), lax.axis_index("sy"), lax.axis_index("ta")
+    plane = nx * ny
+    me = ix * ny + iy
+    rows3, lanes = chunk_ref.shape[1:]
+    snaps = rows3 // 3
+    cells_x = lanes // quarter
+
+    def plane_peer(j):
+        t = lax.rem(me + j, plane)
+        return t, (t // ny, lax.rem(t, ny), it)
+
+    def ta_peer(d):
+        t = lax.rem(it + d, nt)
+        return t, (ix, iy, t)
+
+    def copy(src, dst, sems, index, device):
+        return pltpu.make_async_remote_copy(
+            src_ref=src, dst_ref=dst, send_sem=sems.at[0, index], recv_sem=sems.at[1, index],
+            device_id=device, device_id_type=MESH,
+        )
+
+    barrier = pltpu.get_barrier_semaphore()
+
+    def greet(device):
+        pl.semaphore_signal(barrier, inc=1, device_id=device, device_id_type=MESH)
+
+    loop(1, plane, lambda j: greet(plane_peer(j)[1]))
+    for d in range(1, nt):
+        greet(ta_peer(d)[1])
+    right_ok, left_ok = iy + 1 < ny, iy > 0
+    first, last = it == 0, it == nt - 1
+
+    @pl.when(jnp.logical_and(right_ok, it > 0))
+    def _():
+        greet((ix, iy + 1, 0))
+
+    @pl.when(jnp.logical_and(left_ok, it < nt - 1))
+    def _():
+        greet((ix, iy - 1, nt - 1))
+
+    @pl.when(jnp.logical_and(left_ok, first))
+    def _():
+        for b in range(1, nt):
+            greet((ix, iy - 1, b))
+
+    @pl.when(jnp.logical_and(right_ok, last))
+    def _():
+        for b in range(nt - 1):
+            greet((ix, iy + 1, b))
+
+    extra = (
+        jnp.where(right_ok, jnp.where(last, nt - 1, 0) + jnp.where(it > 0, 1, 0), 0)
+        + jnp.where(left_ok, jnp.where(first, nt - 1, 0) + jnp.where(it < nt - 1, 1, 0), 0)
+    )
+    pl.semaphore_wait(barrier, plane - 1 + nt - 1 + extra)
+
+    def chunk_copy(d, arriving=False):
+        t, device = ta_peer(d)
+        slot = lax.rem(it - d + nt, nt) if arriving else it
+        return copy(chunk_ref.at[t], held.at[slot], chunk_sems, d, device)
+
+    for d in range(1, nt):
+        chunk_copy(d).start()
+    held[it] = chunk_ref[it]
+
+    row, lane = iotas(16, lanes)
+    column = jnp.where(
+        row < cells_x, row * quarter, (row - cells_x) * quarter + quarter - 1
+    )
+    column = jnp.where(row < 2 * cells_x, column, -1)
+    select = (lane == column).astype(jnp.float32).astype(jnp.bfloat16)
+    for q in range(nt):
+        edges[q] = dot16(select, chunk_ref[q], (1, 1)).astype(jnp.bfloat16)
+
+    def left_copy(d):
+        q, device = ta_peer(d)
+        return q > 0, copy(edges.at[jnp.maximum(q - 1, 0)], from_left.at[it], y_sems, d, device)
+
+    def right_copy(d):
+        q, device = ta_peer(d)
+        return q < nt - 1, copy(
+            edges.at[jnp.minimum(q + 1, nt - 1)], from_right.at[it], y_sems, nt + d, device
+        )
+
+    def rim_copies():
+        up = (ix, jnp.minimum(iy + 1, ny - 1), 0)
+        down = (ix, jnp.maximum(iy - 1, 0), nt - 1)
+        return (
+            (right_ok, copy(edges.at[nt - 1], from_left.at[it], rim_sems, it, up)),
+            (left_ok, copy(edges.at[0], from_right.at[it], rim_sems, nt + it, down)),
+        )
+
+    def each_edge(act):
+        for d in range(1, nt):
+            for cond, c in (left_copy(d), right_copy(d)):
+                pl.when(cond)(functools.partial(act, c))
+        for cond, c in rim_copies():
+            pl.when(cond)(functools.partial(act, c))
+
+    each_edge(lambda c: c.start())
+
+    @pl.when(it > 0)
+    def _():
+        from_left[it] = edges[jnp.maximum(it - 1, 0)]
+
+    @pl.when(it < nt - 1)
+    def _():
+        from_right[it] = edges[jnp.minimum(it + 1, nt - 1)]
+
+    @pl.when(jnp.logical_and(first, jnp.logical_not(left_ok)))
+    def _():
+        from_left[...] = jnp.zeros_like(from_left)
+
+    @pl.when(jnp.logical_and(last, jnp.logical_not(right_ok)))
+    def _():
+        from_right[...] = jnp.zeros_like(from_right)
+
+    def x_copies(d):
+        b = lax.rem(it - d + nt, nt)
+        up = (jnp.minimum(ix + 1, nx - 1), iy, it)
+        down = (jnp.maximum(ix - 1, 0), iy, it)
+        return (
+            (ix < nx - 1, copy(held.at[b, :, pl.ds(lanes - 128, 128)], from_up.at[b], x_sems, d, up)),
+            (ix > 0, copy(held.at[b, :, pl.ds(0, 128)], from_down.at[b], x_sems, nt + d, down)),
+        )
+
+    @pl.when(ix == 0)
+    def _():
+        from_up[...] = jnp.zeros_like(from_up)
+
+    @pl.when(ix == nx - 1)
+    def _():
+        from_down[...] = jnp.zeros_like(from_down)
+
+    for d in range(nt):
+        if d:
+            chunk_copy(d, True).wait_recv()
+        for cond, c in x_copies(d):
+            pl.when(cond)(functools.partial(lambda c: c.start(), c))
+
+    row, lane = iotas(lanes, lanes)
+    gap = row - lane
+    same = row // quarter == lane // quarter
+    both = jnp.concatenate(
         [
-            diff_x(comp_u),
-            diff_y(comp_v),
-            0.5 * (diff_y(comp_u) + diff_x(comp_v)),
-            0.5 * diff_x(comp_w),
-            0.5 * diff_y(comp_w),
+            signed_half(gap == quarter, gap == -quarter),
+            signed_half((gap == 1) & same, (gap == -1) & same),
         ],
         axis=1,
     )
-    return fields.reshape(fields.shape[0], -1)
+    row, lane = iotas(128, lanes)
+    none = row < 0
+    above = signed_half(none, (row - (128 - quarter) == lane) & (row >= 128 - quarter))
+    below = signed_half((lane - (lanes - quarter) == row) & (row < quarter), none)
+    row, lane = iotas(16, lanes)
+    none = row < 0
+    left = signed_half(
+        none, (row >= cells_x) & (row < 2 * cells_x) & (lane == (row - cells_x) * quarter)
+    )
+    right = signed_half((row < cells_x) & (lane == row * quarter + quarter - 1), none)
+
+    @pl.when(it > 0)
+    def _():
+        for d in range(1, nt):
+            b = lax.rem(it - d + nt, nt)
+            copy(edges.at[0], from_left.at[b], y_sems, d, (ix, iy, b)).wait_recv()
+
+    @pl.when(it < nt - 1)
+    def _():
+        for d in range(1, nt):
+            b = lax.rem(it - d + nt, nt)
+            copy(edges.at[0], from_right.at[b], y_sems, nt + d, (ix, iy, b)).wait_recv()
+
+    @pl.when(jnp.logical_and(first, left_ok))
+    def _():
+        for b in range(nt):
+            copy(edges.at[0], from_left.at[b], rim_sems, b, (ix, iy - 1, b)).wait_recv()
+
+    @pl.when(jnp.logical_and(last, right_ok))
+    def _():
+        for b in range(nt):
+            copy(edges.at[0], from_right.at[b], rim_sems, nt + b, (ix, iy + 1, b)).wait_recv()
+
+    @pl.when(ix > 0)
+    def _():
+        for d in range(nt):
+            b = lax.rem(it - d + nt, nt)
+            copy(
+                held.at[b, :, pl.ds(lanes - 128, 128)], from_up.at[b], x_sems, d, (ix - 1, iy, it)
+            ).wait_recv()
+
+    @pl.when(ix < nx - 1)
+    def _():
+        for d in range(nt):
+            b = lax.rem(it - d + nt, nt)
+            copy(
+                held.at[b, :, pl.ds(0, 128)], from_down.at[b], x_sems, nt + d, (ix + 1, iy, it)
+            ).wait_recv()
+
+    for b in range(nt):
+        inner = dot16(held[b], both)
+        dx = inner[:, :lanes] + dot16(from_up[b], above) + dot16(from_down[b], below)
+        dy = inner[:, lanes:] + dot16(from_left[b], left, (0, 0)) + dot16(from_right[b], right, (0, 0))
+        ux, vx, wx = (dx[i * snaps : (i + 1) * snaps] for i in range(3))
+        uy, vy, wy = (dy[i * snaps : (i + 1) * snaps] for i in range(3))
+        for k, field in enumerate((ux, vy, 0.5 * (uy + vx), 0.5 * wx, 0.5 * wy)):
+            strain_ref[b * snaps : (b + 1) * snaps, k * lanes : (k + 1) * lanes] = field
+
+    strain = strain_ref[...]
+    coarse = strain.astype(jnp.bfloat16)
+    fine = (strain - coarse.astype(jnp.float32)).astype(jnp.bfloat16)
+    half = nt * snaps // 2
+    blocks = []
+    for a, b in ((0, 0), (1, 0), (1, 1)):
+        ra, rb = slice(a * half, (a + 1) * half), slice(b * half, (b + 1) * half)
+        blocks.append(
+            dot16(coarse[ra], coarse[rb], (1, 1))
+            + (dot16(coarse[ra], fine[rb], (1, 1)) + dot16(fine[ra], coarse[rb], (1, 1)))
+        )
+    share = parts.shape[1]
+    spare = plane * share - 3 * half
+    if spare:
+        blocks.append(jnp.zeros((spare, 128), jnp.float32))
+    parts[...] = jnp.concatenate(blocks, axis=0).reshape(plane, share, 128)
+
+    def scatter_copy(j):
+        t, device = plane_peer(j)
+        return copy(parts.at[t], landed.at[j], scatter_sems, j, device)
+
+    loop(1, plane, lambda j: scatter_copy(j).start())
+    landed[0] = parts[me]
+    loop(1, plane, lambda j: scatter_copy(j).wait_recv())
+    slices[it] = jnp.sum(landed[...], axis=0)
+
+    for d in range(1, nt):
+        copy(slices.at[it], slices.at[it], line_sems, d, ta_peer(d)[1]).start()
+    for d in range(1, nt):
+        b = lax.rem(it - d + nt, nt)
+        copy(slices.at[it], slices.at[b], line_sems, d, ta_peer(d)[1]).wait_recv()
+    whole[me] = jnp.sum(slices[...], axis=0)
+
+    loop(1, plane, lambda j: copy(whole.at[me], whole.at[me], spread_sems, j, plane_peer(j)[1]).start())
+
+    def arrive(j):
+        t = lax.rem(me - j + plane, plane)
+        copy(whole.at[me], whole.at[t], spread_sems, j, plane_peer(j)[1]).wait_recv()
+
+    loop(1, plane, arrive)
+    gram_ref[...] = whole[...].reshape(plane * share, 128)
+
+    for d in range(1, nt):
+        chunk_copy(d).wait_send()
+        copy(slices.at[it], slices.at[it], line_sems, d, ta_peer(d)[1]).wait_send()
+    each_edge(lambda c: c.wait_send())
+    for d in range(nt):
+        for cond, c in x_copies(d):
+            pl.when(cond)(functools.partial(lambda c: c.wait_send(), c))
+    loop(1, plane, lambda j: scatter_copy(j).wait_send())
+    loop(1, plane, lambda j: copy(whole.at[me], whole.at[me], spread_sems, j, plane_peer(j)[1]).wait_send())
 
 
 def local(velocity, seeds_first, seeds_merge):
-    width = seeds_first.shape[0]
-    cells_x = velocity.shape[2]
-    cells_y = velocity.shape[3]
-    blocks = lax.axis_size("ta")
-    quarter = cells_y // blocks
-    rimmed = padded_2(velocity, (("sx", 2), ("sy", 3)), 1)
-    pieces = jnp.stack(
-        [rimmed[..., i * quarter : (i + 1) * quarter + 2] for i in range(blocks)], axis=0
-    )
-    pieces = lax.all_to_all(pieces, "ta", 0, 0, tiled=True)
-    pieces = pieces.transpose(1, 0, 2, 3, 4).reshape(
-        3, blocks * width, cells_x + 2, quarter + 2
-    )
-    strain = strain_rows(pieces.astype(jnp.float32))
-    gram = lax.psum(jnp.dot(strain, strain.T, precision=HI), ("sx", "sy", "ta"))
+    comps, width, cells_x, cells_y = velocity.shape
+    nx, ny, nt = (lax.axis_size(a) for a in ("sx", "sy", "ta"))
+    quarter = cells_y // nt
+    lanes = cells_x * quarter
+    plane = nx * ny
+    share = -(-3 * 2 * width // (8 * plane)) * 8
+    chunks = velocity.reshape(comps, width, cells_x, nt, quarter).transpose(3, 0, 1, 2, 4)
+    chunks = chunks.reshape(nt, comps * width, lanes)
+    rows3 = comps * width
     vmem = pl.BlockSpec(memory_space=pltpu.VMEM)
+    b16, f32 = jnp.bfloat16, jnp.float32
+    dma = pltpu.SemaphoreType.DMA
+    strain, gram = pl.pallas_call(
+        functools.partial(gather_kernel, quarter, nx, ny, nt),
+        out_shape=(
+            jax.ShapeDtypeStruct((nt * width, 5 * lanes), f32),
+            jax.ShapeDtypeStruct((plane * share, 128), f32),
+        ),
+        in_specs=[vmem],
+        out_specs=(vmem, vmem),
+        scratch_shapes=[
+            pltpu.VMEM((nt, rows3, lanes), b16),
+            pltpu.VMEM((nt, rows3, 128), b16),
+            pltpu.VMEM((nt, rows3, 128), b16),
+            pltpu.VMEM((nt, 16, rows3), b16),
+            pltpu.VMEM((nt, 16, rows3), b16),
+            pltpu.VMEM((nt, 16, rows3), b16),
+            pltpu.VMEM((plane, share, 128), f32),
+            pltpu.VMEM((plane, share, 128), f32),
+            pltpu.VMEM((nt, share, 128), f32),
+            pltpu.VMEM((plane, share, 128), f32),
+            dma((2, nt)),
+            dma((2, 2 * nt)),
+            dma((2, 2 * nt)),
+            dma((2, 2 * nt)),
+            dma((2, plane)),
+            dma((2, nt)),
+            dma((2, plane)),
+        ],
+        compiler_params=pltpu.CompilerParams(
+            collective_id=0, has_side_effects=True, vmem_limit_bytes=32 * 2**20
+        ),
+        name="gather",
+    )(chunks)
     out = pl.pallas_call(
         tree_kernel,
-        out_shape=jax.ShapeDtypeStruct((width, strain.shape[1]), jnp.float32),
+        out_shape=jax.ShapeDtypeStruct((width, 5 * lanes), f32),
         in_specs=[vmem] * 4,
         out_specs=vmem,
         compiler_params=pltpu.CompilerParams(vmem_limit_bytes=32 * 2**20),

time: 213 us -> 49.3 us (0.23)
  waiting for transfers between devices: 132 us -> 0 us
  Pallas kernels: 10.4 us -> 45.1 us
  blocking collectives: 32.6 us -> 0 us
  between operations: 13.6 us -> 0.08 us
  starting transfers between devices: 8.74 us -> 0 us
  local copies, waits for them, and re-layouts: 10.4 us -> 3.92 us
  matrix products: 2.95 us -> 0 us
    psum x1 -> x0, waiting for transfers between devices: 123 us -> none  [local(): gram = lax.psum(jnp.dot(strain, strain.T, precision=HI), ('sx', 'sy', 'ta'))]
    pallas_call x1 -> x2, Pallas kernels: 10.4 us -> 45.1 us  [the longest x1 34.5 us: local(): pl.pallas_call(functools.partial(gather_kernel, quarter, nx, ny, nt), out...]
    all_to_all x1 -> x0, blocking collectives: 32.6 us -> none  [local(): pieces = lax.all_to_all(pieces, 'ta', 0, 0, tiled=True)]
    ppermute x4 -> x0, waiting for transfers between devices: 9.05 us -> none  [the longest x2 8.18 us: padded_2(): after = lax.ppermute(leading, axis, down)]
    ppermute x4 -> x0, starting transfers between devices: 8.74 us -> none  [the longest x2 6.16 us: padded_2(): before = lax.ppermute(last, axis, up)]
    slice x6 -> x0, local copies, waits for them, and re-layouts: 5.31 us -> none  [the longest x2 1.73 us: strain_rows(): comp_w = padded[2]]
    dot_general x1 -> x0, matrix products: 2.95 us -> none  [local(): gram = lax.psum(jnp.dot(strain, strain.T, precision=HI), ('sx', 'sy', 'ta'))]
    reshape x1 -> x3, local copies, waits for them, and re-layouts: 0.4 us -> 2.69 us  [the longest x2 2.22 us: local(): velocity.reshape(comps, width, cells_x, nt, quarter)]
  transfers between devices with their start and end apart: 5 -> 0, of which waited for: 4 -> 0; matrix products, arithmetic and copies ran while one was open for 0% -> 0% of each run, Pallas kernels for 0% -> 0%
where the time goes in v2:
time: 49.3 us; the launch traced here: 49.2 us
  Pallas kernels  45.1 us (91%)
  local copies, waits for them, and re-layouts  3.92 us (8%)
    pallas_call x1, Pallas kernels, local(): pl.pallas_call(functools.partial(gather_kernel, quarter, nx, ny, nt), out...  34.5 us
    pallas_call x1, Pallas kernels, local(): pl.pallas_call(tree_kernel, out_shape=jax.ShapeDtypeStruct((width, 5 * la...  10.7 us
    reshape x2, local copies, waits for them, and re-layouts, local(): velocity.reshape(comps, width, cells_x, nt, quarter)  2.22 us
    reshape x1, local copies, waits for them, and re-layouts, local(): return out.reshape(width, 5, cells_x, quarter)  1.13 us

profile of v2, /device:TPU:0, one launch (start us, length us, event | category | flops | bytes accessed | tf_op | source)
XLA Modules:
  0.0 49.2 jit_solution(4445152752538687836)
XLA Ops:
  0.0 1.9 %reshape.9 = bf16[3,64,4,4,64]{4,3,2,1,0:T(4,128)(2,1)S(1)} reshape(bf16[3,64,4,256]{3,2,1,0:T(4,128)(2,1)} %param.3) | data formatting | bytes 786432 | tf_op jit(solution)/shard_map/reshape | solution.py:437
  1.9 0.0 copy-start.1
  1.9 0.0 copy-start
  1.9 0.3 copy.7
  2.3 0.5 reshape.10.chunk_ref
  2.7 34.5 %gather.1 = (f32[256,1280]{1,0:T(8,128)S(1)}, f32[384,128]{1,0:T(8,128)S(1)}) custom-call(bf16[4,192,256]{2,1,0:T(8,128)(2,1)S(1)} %reshape.10.chunk_ref), custom_call_target="tpu_custom_call" | custom-call | tf_op jit(solution)/shard_map/gather/pallas_call | solution.py:443
  37.2 0.0 copy-done.1
  37.2 0.1 copy.5.merge_ref
  37.3 0.0 copy-done
  37.3 10.7 %tree.1 = f32[64,1280]{1,0:T(8,128)S(1)} custom-call(f32[384,128]{1,0:T(8,128)S(1)} %get-tuple-element.7.gram_ref, f32[256,1280]{1,0:T(8,128)S(1)} %get-tuple-element.8.strain_ref, s32[64,64]{1,0:T(8,128)S(1)} %copy-done, s32[2,128,64]{2,1,0:T(8,128)S(1)} %copy.5.merge_ref), custom_call_target="tpu_custom_call" | custom-call | tf_op jit(solution)/shard_map/tree/pallas_call | solution.py:475
  48.0 1.1 %reshape.11 = f32[64,5,4,64]{3,2,1,0:T(4,128)} reshape(f32[64,1280]{1,0:T(8,128)S(1)} %tree.1) | data formatting | bytes 655360 | tf_op jit(solution)/shard_map/reshape | solution.py:483
Async XLA Ops:
  1.9 35.3 %copy-start.1 = (s32[2,128,64]{1,2,0:T(8,128)S(1)}, s32[2,128,64]{1,2,0:T(8,128)}, u32[]{:S(2)}) copy-start(s32[2,128,64]{1,2,0:T(8,128)} %param.5) | copy-start | bytes 196612
  1.9 35.4 %copy-start = (s32[64,64]{1,0:T(8,128)S(1)}, s32[64,64]{1,0:T(8,128)}, u32[]{:S(2)}) copy-start(s32[64,64]{1,0:T(8,128)} %first_ref.1) | copy-start | bytes 49156

commit v3 on v2

--- a/solution.py
+++ b/solution.py
@@ -162,8 +162,8 @@
 
 def gather_kernel(
     quarter, nx, ny, nt,
-    chunk_ref, strain_ref, gram_ref,
-    held, from_up, from_down, edges, from_left, from_right, parts, landed, slices, whole,
+    velocity_ref, strain_ref, gram_ref,
+    chunk_ref, held, from_up, from_down, edges, from_left, from_right, parts, landed, slices, whole,
     chunk_sems, x_sems, y_sems, rim_sems, scatter_sems, line_sems, spread_sems,
 ):
     ix, iy, it = lax.axis_index("sx"), lax.axis_index("sy"), lax.axis_index("ta")
@@ -220,6 +220,13 @@
         jnp.where(right_ok, jnp.where(last, nt - 1, 0) + jnp.where(it > 0, 1, 0), 0)
         + jnp.where(left_ok, jnp.where(first, nt - 1, 0) + jnp.where(it < nt - 1, 1, 0), 0)
     )
+
+    for c in range(3):
+        field = velocity_ref[c].astype(jnp.float32)
+        rows = [field[:, x, :] for x in range(cells_x)]
+        for q in range(nt):
+            piece = jnp.concatenate([r[:, q * quarter : (q + 1) * quarter] for r in rows], axis=1)
+            chunk_ref[q, c * snaps : (c + 1) * snaps] = piece.astype(jnp.bfloat16)
     pl.semaphore_wait(barrier, plane - 1 + nt - 1 + extra)
 
     def chunk_copy(d, arriving=False):
@@ -434,8 +441,6 @@
     lanes = cells_x * quarter
     plane = nx * ny
     share = -(-3 * 2 * width // (8 * plane)) * 8
-    chunks = velocity.reshape(comps, width, cells_x, nt, quarter).transpose(3, 0, 1, 2, 4)
-    chunks = chunks.reshape(nt, comps * width, lanes)
     rows3 = comps * width
     vmem = pl.BlockSpec(memory_space=pltpu.VMEM)
     b16, f32 = jnp.bfloat16, jnp.float32
@@ -449,6 +454,7 @@
         in_specs=[vmem],
         out_specs=(vmem, vmem),
         scratch_shapes=[
+            pltpu.VMEM((nt, rows3, lanes), b16),
             pltpu.VMEM((nt, rows3, lanes), b16),
             pltpu.VMEM((nt, rows3, 128), b16),
             pltpu.VMEM((nt, rows3, 128), b16),
@@ -471,7 +477,7 @@
             collective_id=0, has_side_effects=True, vmem_limit_bytes=32 * 2**20
         ),
         name="gather",
-    )(chunks)
+    )(velocity)
     out = pl.pallas_call(
         tree_kernel,
         out_shape=jax.ShapeDtypeStruct((width, 5 * lanes), f32),

time: 49.3 us -> 49.1 us (level)
    reshape x3 -> x0, local copies, waits for them, and re-layouts: 2.69 us -> none  [the longest x2 2.22 us: local(): velocity.reshape(comps, width, cells_x, nt, quarter)]
    unnamed x5, local copies, waits for them, and re-layouts: 0.11 us -> 2.68 us
where the time goes in v3:
time: 49.1 us; the launch traced here: 48.8 us
  Pallas kernels  45 us (92%)
  local copies, waits for them, and re-layouts  3.8 us (8%)
    pallas_call x1, Pallas kernels, local(): pl.pallas_call(functools.partial(gather_kernel, quarter, nx, ny, nt), out...  34.3 us
    pallas_call x1, Pallas kernels, local(): pl.pallas_call(tree_kernel, out_shape=jax.ShapeDtypeStruct((width, 5 * la...  10.7 us
    unnamed x5, local copies, waits for them, and re-layouts  2.68 us
    reshape x1, local copies, waits for them, and re-layouts, local(): return out.reshape(width, 5, cells_x, quarter)  1.13 us

profile of v3, /device:TPU:0, one launch (start us, length us, event | category | flops | bytes accessed | tf_op | source)
XLA Modules:
  0.0 48.8 jit_solution(2943508974476397232)
XLA Ops:
  0.0 0.9 %copy.4.merge_ref = s32[2,128,64]{2,1,0:T(8,128)S(1)} copy(s32[2,128,64]{1,2,0:T(8,128)} %param.5) | data formatting | bytes 131072 | tf_op args[2]
  0.9 0.0 copy-start
  1.0 1.0 %copy-done = bf16[3,64,4,256]{3,2,1,0:T(4,128)(2,1)S(1)} copy-done((bf16[3,64,4,256]{3,2,1,0:T(4,128)(2,1)S(1)}, bf16[3,64,4,256]{3,2,1,0:T(4,128)(2,1)}, u32[]{:S(2)}) %copy-start) | copy-done | bytes 393240
  1.9 34.3 %gather.1 = (f32[256,1280]{1,0:T(8,128)S(1)}, f32[384,128]{1,0:T(8,128)S(1)}) custom-call(bf16[3,64,4,256]{3,2,1,0:T(4,128)(2,1)S(1)} %copy-done), custom_call_target="tpu_custom_call" | custom-call | tf_op jit(solution)/shard_map/gather/pallas_call | solution.py:448
  36.2 0.0 copy-start.1
  36.2 0.7 %copy-done.1 = s32[64,64]{1,0:T(8,128)S(1)} copy-done((s32[64,64]{1,0:T(8,128)S(1)}, s32[64,64]{1,0:T(8,128)}, u32[]{:S(2)}) %copy-start.1) | copy-done | bytes 16408
  37.0 10.7 %tree.1 = f32[64,1280]{1,0:T(8,128)S(1)} custom-call(f32[384,128]{1,0:T(8,128)S(1)} %get-tuple-element.7.gram_ref, f32[256,1280]{1,0:T(8,128)S(1)} %get-tuple-element.8.strain_ref, s32[64,64]{1,0:T(8,128)S(1)} %copy-done.1, s32[2,128,64]{2,1,0:T(8,128)S(1)} %copy.4.merge_ref), custom_call_target="tpu_custom_call" | custom-call | tf_op jit(solution)/shard_map/tree/pallas_call | solution.py:481
  47.7 1.1 %reshape.3 = f32[64,5,4,64]{3,2,1,0:T(4,128)} reshape(f32[64,1280]{1,0:T(8,128)S(1)} %tree.1) | data formatting | bytes 655360 | tf_op jit(solution)/shard_map/reshape | solution.py:489
Async XLA Ops:
  0.9 1.0 %copy-start = (bf16[3,64,4,256]{3,2,1,0:T(4,128)(2,1)S(1)}, bf16[3,64,4,256]{3,2,1,0:T(4,128)(2,1)}, u32[]{:S(2)}) copy-start(bf16[3,64,4,256]{3,2,1,0:T(4,128)(2,1)} %velocity_ref.1) | copy-start | bytes 1179652
  36.2 0.8 %copy-start.1 = (s32[64,64]{1,0:T(8,128)S(1)}, s32[64,64]{1,0:T(8,128)}, u32[]{:S(2)}) copy-start(s32[64,64]{1,0:T(8,128)} %first_ref.1) | copy-start | bytes 49156
